TPU v7x, 32 devices: a whole 2x2x4 slice. The times are simulated.
32 devices in a mesh: src: 4 (over y, x), tgt: 8 (over z, core).
Axes of the slice: x: 2, y: 2, z: 4, core: 2. Of those that a mesh axis runs over, the one named last changes fastest.
Arguments:
- tile_cost: bfloat16 [384, 512, 512], P(('src', 'tgt')), may hold values from -2.5 to 7.5
- tile_pairs: int32 [384, 2], P(('src', 'tgt')), may hold values from 0 to 95, as said below
- tile_counts: int32 [32], P(('src', 'tgt')), may hold values from 3 to 12, as said below
- src_mass: float32 [12288], P('src'), may hold values from 0.25 to 4
- tgt_mass: float32 [49152], P('tgt'), may hold values from 0.25 to 4
- targets_t: bfloat16 [64, 49152], P(None, 'tgt'), may hold values from -18 to 18
Outputs:
- mapped_t: float32 [64, 12288], P(None, ('src', 'tgt'))
Inputs may be any that keep to these rules, and one draw needn't show every extreme that they name: `tile_pairs`: device d of the src+tgt order owns slots d * 12 to (d + 1) * 12 - 1. Its first tile_counts[d] slots hold distinct kept pairs whose source tile lies among its src index's 6 tiles and whose target tile among its tgt index's 12 tiles; its other slots repeat its first slot. Every source tile is in exactly 8 kept pairs, every target tile in at least one. `tile_counts`: over the devices of one src index the counts sum to 48; some device of every src index holds 12; every device holds at least (8 * 6 - 12) // (8 - 1) - 2.
All inputs are finite; a program needn't handle non-finite values.
Results may differ from a plain program's by a relative error of at most 0.0029.
Values may be sent and summed in bfloat16 or wider, within the bound.
A program may use at most 64 MiB of HBM per device.

v0:
```python
import functools

import jax
import jax.numpy as jnp
from jax import lax
from jax.experimental import pallas as pl
from jax.experimental.pallas import tpu as pltpu
from jax.sharding import PartitionSpec as P

MESH = pl.DeviceIdType.MESH
inverse_eps = 50.0 * 1.4426950408889634
negative_floor = -1e30
ROWS = 64
LANES = 128
PAD = 16


def logsumexp0(parts):
    top = jnp.max(parts, axis=0)
    return top + jnp.log2(jnp.sum(jnp.exp2(parts - top[None]), axis=0))


def kernel(
    n_src,
    n_tgt,
    pairs_ref,
    count_ref,
    cost_hbm,
    src_mass_flat,
    tgt_mass_flat,
    targets_hbm,
    out_ref,
    cost,
    q,
    low,
    tgts,
    prods,
    slot_cols,
    slot_rows,
    pad_rows,
    row_pot,
    col_stab,
    col_sum,
    col_fac,
    tgt_pot,
    src_mass_ref,
    tgt_mass_ref,
    row_buf1,
    row_buf2,
    col_buf1,
    col_buf2,
    out_part,
    pair_recv,
    out_send,
    out_recv,
    mass_send,
    mass_recv,
    cost_sem,
    tgts_sem,
    row_send1,
    row_recv1,
    row_send2,
    row_recv2,
    col_send1,
    col_recv1,
    col_send2,
    col_recv2,
    pair_send_sem,
    pair_recv_sem,
    out_send_sem,
    out_recv_sem,
):
    cap, edge = cost.shape[0], cost.shape[1]
    src_tiles, tgt_tiles = src_mass_ref.shape[0], tgt_mass_ref.shape[0]
    dim = targets_hbm.shape[0]
    my_src, my_tgt = lax.axis_index("src"), lax.axis_index("tgt")
    chunks = edge // ROWS

    for k in range(cap):
        pltpu.make_async_copy(cost_hbm.at[k], cost.at[k], cost_sem.at[k]).start()
    for t in range(tgt_tiles):
        pltpu.make_async_copy(
            targets_hbm.at[:, pl.ds(t * edge, edge)], tgts.at[t, pl.ds(0, dim)], tgts_sem.at[t]
        ).start()

    barrier = pltpu.get_barrier_semaphore()
    for off in range(1, n_tgt):
        pl.semaphore_signal(
            barrier, inc=1, device_id={"tgt": lax.rem(my_tgt + off, n_tgt)}, device_id_type=MESH
        )
    for off in range(1, n_src):
        pl.semaphore_signal(
            barrier, inc=1, device_id={"src": lax.rem(my_src + off, n_src)}, device_id_type=MESH
        )

    pad_rows[...] = jnp.zeros_like(pad_rows)
    slot_cols[...] = jnp.zeros_like(slot_cols)
    tgts[:, dim:, :] = jnp.ones((tgt_tiles, PAD, edge), jnp.bfloat16)

    for s in range(src_tiles):
        src_mass_ref[s : s + 1, :] = src_mass_flat[s * edge : (s + 1) * edge].reshape(1, edge)
    for t in range(tgt_tiles):
        tgt_mass_ref[t : t + 1, :] = tgt_mass_flat[t * edge : (t + 1) * edge].reshape(1, edge)

    count = count_ref[0]
    src_of = [lax.rem(pairs_ref[0, k], src_tiles) for k in range(cap)]
    tgt_of = [lax.rem(pairs_ref[1, k], tgt_tiles) for k in range(cap)]
    src_id = [jnp.where(k < count, src_of[k], -1) for k in range(cap)]
    tgt_id = [jnp.where(k < count, tgt_of[k], -1) for k in range(cap)]
    src_rows = lax.broadcasted_iota(jnp.int32, (src_tiles, edge), 0)
    tgt_rows = lax.broadcasted_iota(jnp.int32, (tgt_tiles, edge), 0)
    lane = lax.broadcasted_iota(jnp.int32, (ROWS, LANES), 1)

    def wide(block):
        return jnp.concatenate([block] * (edge // LANES), axis=1)

    def put_column(k, c, value):
        rows = slice(c * ROWS, (c + 1) * ROWS)
        slot_cols[rows, :] = jnp.where(lane == k, value, slot_cols[rows, :])

    def slots_as_rows():
        slot_rows[...] = slot_cols[...].T[:PAD]

    def spread_rows(values):
        pad_rows[0:src_tiles, :] = values
        columns = pad_rows[...].T
        for s in range(src_tiles):
            row_pot[s] = jnp.broadcast_to(columns[:, s : s + 1], (edge, LANES))

    def exchange(buf, axis, me, n, send_sem, recv_sem):
        copies = []
        for off in range(1, n):
            copy = pltpu.make_async_remote_copy(
                src_ref=buf.at[0],
                dst_ref=buf.at[off],
                send_sem=send_sem.at[off - 1],
                recv_sem=recv_sem.at[off - 1],
                device_id={axis: lax.rem(me + off, n)},
                device_id_type=MESH,
            )
            copy.start()
            copies.append(copy)
        for copy in copies:
            copy.wait()

    def merge_logs(parts, ids, rows):
        top = jnp.full(rows.shape, negative_floor, jnp.float32)
        for part, tile in zip(parts, ids):
            top = jnp.maximum(top, jnp.where(rows == tile, part, negative_floor))
        total = jnp.zeros(rows.shape, jnp.float32)
        for part, tile in zip(parts, ids):
            total = total + jnp.where(rows == tile, jnp.exp2(part - top), 0.0)
        return jnp.where(total > 0.0, top + jnp.log2(total), negative_floor)

    def merge_sums(parts, ids, rows):
        total = jnp.zeros(rows.shape, jnp.float32)
        for part, tile in zip(parts, ids):
            total = total + jnp.where(rows == tile, part, 0.0)
        return total

    def halves(combine, block):
        parts = [block[:, at : at + LANES] for at in range(0, edge, LANES)]
        return functools.reduce(combine, parts)

    def in_pairs(step):
        def both(i, carry):
            step(2 * i)
            step(2 * i + 1)
            return carry

        lax.fori_loop(0, cap // 2, both, 0)

    def row_first(i, carry):
        for u in range(2):
            k = 2 * i + u
            pltpu.make_async_copy(cost_hbm.at[k], cost.at[k], cost_sem.at[k]).wait()
            for c in range(chunks):
                rows = slice(c * ROWS, (c + 1) * ROWS)
                tile = cost[k, rows, :].astype(jnp.float32) * inverse_eps
                q[k, rows, :] = tile
                least = jnp.min(halves(jnp.minimum, tile), axis=1, keepdims=True)
                low[u, rows, :] = jnp.broadcast_to(least, (ROWS, LANES))
        for u in range(2):
            k = 2 * i + u
            for c in range(chunks):
                rows = slice(c * ROWS, (c + 1) * ROWS)
                value = jnp.exp2(wide(low[u, rows, :]) - q[k, rows, :])
                total = jnp.sum(halves(jnp.add, value), axis=1, keepdims=True)
                put_column(k, c, jnp.log2(total) - low[u, rows, :])
        return carry

    lax.fori_loop(0, cap // 2, row_first, 0)
    slots_as_rows()
    row_buf1[0] = merge_logs([slot_rows[k : k + 1, :] for k in range(cap)], src_id, src_rows)
    pl.semaphore_wait(barrier, n_tgt - 1 + n_src - 1)
    exchange(row_buf1, "tgt", my_tgt, n_tgt, row_send1, row_recv1)
    spread_rows(jnp.log2(src_mass_ref[...]) - logsumexp0(row_buf1[...]))

    def col_first(i, carry):
        tops = []
        for u in range(2):
            k = 2 * i + u
            s = lax.rem(pairs_ref[0, k], src_tiles)
            top = jnp.full((8, edge), negative_floor, jnp.float32)
            for c in range(chunks):
                rows = slice(c * ROWS, (c + 1) * ROWS)
                score = wide(row_pot[s, rows, :]) - q[k, rows, :]
                top = jnp.maximum(top, jnp.max(score.reshape(ROWS // 8, 8, edge), axis=0))
            tops.append(jnp.broadcast_to(jnp.max(top, axis=0, keepdims=True), (8, edge)))
        for u in range(2):
            k = 2 * i + u
            s = lax.rem(pairs_ref[0, k], src_tiles)
            total = jnp.zeros((8, edge), jnp.float32)
            for c in range(chunks):
                rows = slice(c * ROWS, (c + 1) * ROWS)
                score = (wide(row_pot[s, rows, :]) - q[k, rows, :]).reshape(ROWS // 8, 8, edge)
                value = jnp.exp2(score - tops[u][None])
                q[k, rows, :] = value.reshape(ROWS, edge)
                total = total + jnp.sum(value, axis=0)
            col_stab[k] = tops[u]
            col_sum[k] = jnp.broadcast_to(jnp.sum(total, axis=0, keepdims=True), (8, edge))
        return carry

    lax.fori_loop(0, cap // 2, col_first, 0)
    col_buf1[0] = merge_logs(
        [col_stab[k, 0:1, :] + jnp.log2(col_sum[k, 0:1, :]) for k in range(cap)], tgt_id, tgt_rows
    )
    exchange(col_buf1, "src", my_src, n_src, col_send1, col_recv1)
    potential = jnp.log2(tgt_mass_ref[...]) - logsumexp0(col_buf1[...])
    for t in range(tgt_tiles):
        tgt_pot[t] = jnp.broadcast_to(potential[t : t + 1, :], (8, edge))

    def row_second(k):
        t = lax.rem(pairs_ref[1, k], tgt_tiles)
        alive = jnp.full((8, edge), k, jnp.int32) < count
        factor = jnp.where(alive, jnp.exp2(tgt_pot[t] + col_stab[k]), 0.0)
        col_fac[k] = factor
        for c in range(chunks):
            rows = slice(c * ROWS, (c + 1) * ROWS)
            value = q[k, rows, :].reshape(ROWS // 8, 8, edge) * factor[None]
            total = halves(jnp.add, value.reshape(ROWS, edge))
            put_column(k, c, jnp.sum(total, axis=1, keepdims=True))

    in_pairs(row_second)
    slots_as_rows()
    row_buf2[0] = merge_sums([slot_rows[k : k + 1, :] for k in range(cap)], src_id, src_rows)
    exchange(row_buf2, "tgt", my_tgt, n_tgt, row_send2, row_recv2)
    spread_rows(src_mass_ref[...] / jnp.sum(row_buf2[...], axis=0))

    def col_second(k):
        s = lax.rem(pairs_ref[0, k], src_tiles)
        total = jnp.zeros((8, edge), jnp.float32)
        for c in range(chunks):
            rows = slice(c * ROWS, (c + 1) * ROWS)
            value = q[k, rows, :] * wide(row_pot[s, rows, :])
            q[k, rows, :] = value
            total = total + jnp.sum(value.reshape(ROWS // 8, 8, edge), axis=0)
        col_sum[k] = jnp.broadcast_to(jnp.sum(total, axis=0, keepdims=True), (8, edge)) * col_fac[k]

    in_pairs(col_second)
    col_buf2[0] = merge_sums([col_sum[k, 0:1, :] for k in range(cap)], tgt_id, tgt_rows)
    exchange(col_buf2, "src", my_src, n_src, col_send2, col_recv2)
    potential = tgt_mass_ref[...] / jnp.sum(col_buf2[...], axis=0)
    for t in range(tgt_tiles):
        tgt_pot[t] = jnp.broadcast_to(potential[t : t + 1, :], (8, edge))

    for t in range(tgt_tiles):
        pltpu.make_async_copy(
            targets_hbm.at[:, pl.ds(t * edge, edge)], tgts.at[t, pl.ds(0, dim)], tgts_sem.at[t]
        ).wait()

    def map_slot(k):
        t = lax.rem(pairs_ref[1, k], tgt_tiles)
        factor = tgt_pot[t] * col_fac[k]
        left = tgts[t]
        for h in range(edge // 256):
            parts = []
            for c in range(256 // ROWS):
                rows = slice(h * 256 + c * ROWS, h * 256 + (c + 1) * ROWS)
                value = q[k, rows, :].reshape(ROWS // 8, 8, edge)
                parts.append((value * factor[None]).reshape(ROWS, edge).astype(jnp.bfloat16))
            prods[k, :, h * 256 : (h + 1) * 256] = lax.dot_general(
                left,
                jnp.concatenate(parts, axis=0),
                (((1,), (1,)), ((), ())),
                preferred_element_type=jnp.float32,
            )

    in_pairs(map_slot)

    share = out_ref.shape[1]
    tall = dim + PAD
    core, layer, layers = lax.rem(my_tgt, 2), my_tgt // 2, n_tgt // 2

    def pair_copy(j):
        return pltpu.make_async_remote_copy(
            src_ref=out_part.at[2 * j + 1 - core],
            dst_ref=pair_recv.at[j],
            send_sem=pair_send_sem.at[j],
            recv_sem=pair_recv_sem.at[j],
            device_id={"tgt": my_tgt + 1 - 2 * core},
            device_id_type=MESH,
        )

    def layer_copies(other, slot):
        return [
            pltpu.make_async_remote_copy(
                src_ref=sent.at[slot],
                dst_ref=landed.at[slot],
                send_sem=out_send_sem.at[kind, slot],
                recv_sem=out_recv_sem.at[kind, slot],
                device_id={"tgt": 2 * other + core},
                device_id_type=MESH,
            )
            for kind, (sent, landed) in enumerate(((out_send, out_recv), (mass_send, mass_recv)))
        ]

    def ship(j):
        @pl.when(layer != j)
        def _():
            slot = lax.rem(j - layer + layers, layers) - 1
            block = 2 * j + core
            pair_copy(j).wait_recv()
            out_send[slot] = (out_part[block, :dim] + pair_recv[j, :dim]).astype(jnp.bfloat16)
            mass_send[slot] = out_part[block, dim : dim + 1] + pair_recv[j, dim : dim + 1]
            for copy in layer_copies(j, slot):
                copy.start()

    picks = [
        [jnp.where(src_id[k] == s, 1.0, 0.0) for k in range(cap)] for s in range(src_tiles)
    ]
    for place in range(0, src_tiles * edge, LANES):
        s, start = place // edge, place % edge
        total = jnp.zeros((tall, LANES), jnp.float32)
        for k in range(cap):
            total = total + prods[k, :, start : start + LANES] * picks[s][k]
        block, start = place // share, place % share
        out_part[block, :, start : start + LANES] = total
        if (place + LANES) % (2 * share) == 0:
            pair_copy(block // 2).start()
            if block > 2:
                ship(block // 2 - 1)
    ship(layers - 1)

    for off in range(1, layers):
        pair_copy(lax.rem(layer + off, layers)).wait_send()
    pair_copy(layer).wait()
    block = 2 * layer + core
    total = out_part[block, :dim] + pair_recv[layer, :dim]
    mass = out_part[block, dim : dim + 1] + pair_recv[layer, dim : dim + 1]
    for off in range(layers - 1):
        for copy in layer_copies(lax.rem(layer + off + 1, layers), off):
            copy.wait()
        total = total + out_recv[off].astype(jnp.float32)
        mass = mass + mass_recv[off]
    out_ref[...] = total / mass


def local(n_src, n_tgt, tile_cost, tile_pairs, tile_counts, src_mass, tgt_mass, targets_t):
    cap, edge = tile_cost.shape[0], tile_cost.shape[1]
    src_tiles, tgt_tiles = src_mass.shape[0] // edge, tgt_mass.shape[0] // edge
    dim = targets_t.shape[0]
    share = src_mass.shape[0] // n_tgt
    tall = dim + PAD
    f32, bf16 = jnp.float32, jnp.bfloat16
    dma = pltpu.SemaphoreType.DMA
    smem = pl.BlockSpec(memory_space=pltpu.SMEM)
    vmem = pl.BlockSpec(memory_space=pltpu.VMEM)
    hbm = pl.BlockSpec(memory_space=pl.ANY)
    return pl.pallas_call(
        functools.partial(kernel, n_src, n_tgt),
        out_shape=jax.ShapeDtypeStruct((dim, share), f32),
        in_specs=[smem, smem, hbm, vmem, vmem, hbm],
        out_specs=vmem,
        scratch_shapes=[
            pltpu.VMEM((cap, edge, edge), bf16),
            pltpu.VMEM((cap, edge, edge), f32),
            pltpu.VMEM((2, edge, LANES), f32),
            pltpu.VMEM((tgt_tiles, tall, edge), bf16),
            pltpu.VMEM((cap, tall, edge), f32),
            pltpu.VMEM((edge, LANES), f32),
            pltpu.VMEM((PAD, edge), f32),
            pltpu.VMEM((LANES, edge), f32),
            pltpu.VMEM((src_tiles, edge, LANES), f32),
            pltpu.VMEM((cap, 8, edge), f32),
            pltpu.VMEM((cap, 8, edge), f32),
            pltpu.VMEM((cap, 8, edge), f32),
            pltpu.VMEM((tgt_tiles, 8, edge), f32),
            pltpu.VMEM((src_tiles, edge), f32),
            pltpu.VMEM((tgt_tiles, edge), f32),
            pltpu.VMEM((n_tgt, src_tiles, edge), f32),
            pltpu.VMEM((n_tgt, src_tiles, edge), f32),
            pltpu.VMEM((n_src, tgt_tiles, edge), f32),
            pltpu.VMEM((n_src, tgt_tiles, edge), f32),
            pltpu.VMEM((n_tgt, tall, share), f32),
            pltpu.VMEM((n_tgt // 2, tall, share), f32),
            pltpu.VMEM((n_tgt // 2 - 1, dim, share), bf16),
            pltpu.VMEM((n_tgt // 2 - 1, dim, share), bf16),
            pltpu.VMEM((n_tgt // 2 - 1, 1, share), f32),
            pltpu.VMEM((n_tgt // 2 - 1, 1, share), f32),
            dma((cap,)),
            dma((tgt_tiles,)),
            dma((n_tgt - 1,)),
            dma((n_tgt - 1,)),
            dma((n_tgt - 1,)),
            dma((n_tgt - 1,)),
            dma((n_src - 1,)),
            dma((n_src - 1,)),
            dma((n_src - 1,)),
            dma((n_src - 1,)),
            dma((n_tgt // 2,)),
            dma((n_tgt // 2,)),
            dma((2, n_tgt // 2 - 1)),
            dma((2, n_tgt // 2 - 1)),
        ],
        compiler_params=pltpu.CompilerParams(
            collective_id=0, has_side_effects=True, vmem_limit_bytes=56 * 1024 * 1024
        ),
    )(
        tile_pairs.T,
        tile_counts,
        tile_cost,
        src_mass,
        tgt_mass,
        targets_t,
    )


def solution(mesh):
    return jax.shard_map(
        functools.partial(local, mesh.shape["src"], mesh.shape["tgt"]),
        mesh=mesh,
        in_specs=(
            P(("src", "tgt"), None, None),
            P(("src", "tgt"), None),
            P(("src", "tgt")),
            P("src"),
            P("tgt"),
            P(None, "tgt"),
        ),
        out_specs=P(None, ("src", "tgt")),
        check_vma=False,
    )
```

profile of v0, /device:TPU:0, one launch (start us, length us, event | category | flops | bytes accessed | tf_op | source)
XLA Modules:
  0.0 45.1 jit_solution(17702233994453227133)
XLA Ops:
  0.7 42.9 %shard_map.64 = f32[64,384]{1,0:T(8,128)} custom-call(s32[2,12]{1,0:T(2,128)} %bitcast.1, s32[1]{0:T(128)S(6)} %copy.8.count_ref, bf16[12,512,512]{2,1,0:T(8,128)(2,1)} %cost_hbm.1, f32[3072]{0:T(1024)} %src_mass_flat.1, f32[6144]{0:T(1024)} %tgt_mass_flat.1, bf16[64,6144]{1,0:T(8,128)(2,1)} %targets_hbm.1), custom_call_target="tpu_custom_call" | custom-call | tf_op jit(solution)/shard_map/pallas_call | solution.py:370
  43.6 1.5 %copy.9 = f32[64,384]{1,0:T(8,128)} copy(f32[64,384]{1,0:T(8,128)} %shard_map.64) | data formatting | bytes 196608
where the time goes:
time: 45.3 us; the launch traced here: 45.1 us
  Pallas kernels  42.9 us (95%)
  local copies, waits for them, and re-layouts  1.54 us (3%)
  between operations  0.66 us (1%)
    pallas_call x1, Pallas kernels, local(): pl.pallas_call(functools.partial(kernel, n_src, n_tgt), out_shape=jax.Sha...  42.9 us
    unnamed x1, local copies, waits for them, and re-layouts  1.54 us

commit v1 on v0

--- a/solution.py
+++ b/solution.py
@@ -201,11 +201,14 @@
         for u in range(2):
             k = 2 * i + u
             s = lax.rem(pairs_ref[0, k], src_tiles)
-            top = jnp.full((8, edge), negative_floor, jnp.float32)
+            top = jnp.full((16, edge), negative_floor, jnp.bfloat16)
             for c in range(chunks):
                 rows = slice(c * ROWS, (c + 1) * ROWS)
-                score = wide(row_pot[s, rows, :]) - q[k, rows, :]
-                top = jnp.maximum(top, jnp.max(score.reshape(ROWS // 8, 8, edge), axis=0))
+                rough = (row_pot[s, rows, :] * (1.0 / inverse_eps)).astype(jnp.bfloat16)
+                rough = (wide(rough) - cost[k, rows, :]).reshape(ROWS // 16, 16, edge)
+                for r in range(ROWS // 16):
+                    top = jnp.maximum(top, rough[r])
+            top = top.astype(jnp.float32) * inverse_eps
             tops.append(jnp.broadcast_to(jnp.max(top, axis=0, keepdims=True), (8, edge)))
         for u in range(2):
             k = 2 * i + u

time: 45.3 us -> 44.4 us (0.980)
  Pallas kernels: 42.9 us -> 42 us
    pallas_call x1, Pallas kernels: 42.9 us -> 42 us  [local(): pl.pallas_call(functools.partial(kernel, n_src, n_tgt), out_shape=jax.Sha...]
where the time goes in v1:
time: 44.4 us; the launch traced here: 44.2 us
  Pallas kernels  42 us (95%)
  local copies, waits for them, and re-layouts  1.54 us (3%)
  between operations  0.66 us (1%)
    pallas_call x1, Pallas kernels, local(): pl.pallas_call(functools.partial(kernel, n_src, n_tgt), out_shape=jax.Sha...  42 us
    unnamed x1, local copies, waits for them, and re-layouts  1.54 us

profile of v1, /device:TPU:0, one launch (start us, length us, event | category | flops | bytes accessed | tf_op | source)
XLA Modules:
  0.0 44.2 jit_solution(14266037491881257176)
XLA Ops:
  0.7 42.0 %shard_map.64 = f32[64,384]{1,0:T(8,128)} custom-call(s32[2,12]{1,0:T(2,128)} %bitcast.1, s32[1]{0:T(128)S(6)} %copy.8.count_ref, bf16[12,512,512]{2,1,0:T(8,128)(2,1)} %cost_hbm.1, f32[3072]{0:T(1024)} %src_mass_flat.1, f32[6144]{0:T(1024)} %tgt_mass_flat.1, bf16[64,6144]{1,0:T(8,128)(2,1)} %targets_hbm.1), custom_call_target="tpu_custom_call" | custom-call | tf_op jit(solution)/shard_map/pallas_call | solution.py:373
  42.7 1.5 %copy.9 = f32[64,384]{1,0:T(8,128)} copy(f32[64,384]{1,0:T(8,128)} %shard_map.64) | data formatting | bytes 196608
